TPU v7x, 32 devices: a whole 2x2x4 slice. The times are simulated.
32 devices in a mesh: grp: 2 (over y), mode: 4 (over z), site: 4 (over x, core).
Axes of the slice: x: 2, y: 2, z: 4, core: 2. Of those that a mesh axis runs over, the one named last changes fastest.
Arguments:
- w_modes: bfloat16 [2, 1024, 12, 256], P(None, ('grp', 'mode'), None, 'site'), parts along dimension 1, may hold values from -6 to 6
- v_modes: bfloat16 [2, 512, 12, 256], P(None, ('grp', 'mode'), None, 'site'), parts along dimension 1, may hold values from -0.078125 to 0.078125
- momenta: int32 [4, 3], replicated, may hold values from -2 to 2
Outputs:
- meson: float32 [2, 4, 1024, 192], P(None, None, ('grp', 'mode', 'site')), parts along dimension 2
There are 2 independent parts, one for each index of `grp`. A program takes and returns all parts, laid end to end along the dimension named above; an argument that names none is the same for every part. Nothing has to cross between parts.
All inputs are finite; a program needn't handle non-finite values.
Results may differ from a plain program's by a relative error of at most 0.0028.
Values may be sent and summed in bfloat16 or wider, within the bound.
A program may use at most 64 MiB of HBM per device.

v0:
```python
import jax
import jax.numpy as jnp
import numpy as np
from jax import lax
from jax.sharding import PartitionSpec as P

LAT = 96
REACH = 4


def shifted(value, axis, steps):
    count = lax.axis_size(axis)
    pairs = [(source, (source + steps) % count) for source in range(count)]
    return lax.ppermute(value, axis, pairs)


def make_phase(momenta, first, count):
    index = first + jnp.arange(count, dtype=jnp.int32)
    xcoord = index % LAT
    ycoord = index // LAT % LAT
    zcoord = index // (LAT * LAT)
    total = (
        momenta[:, 0:1] * xcoord[None, :]
        + momenta[:, 1:2] * ycoord[None, :]
        + momenta[:, 2:3] * zcoord[None, :]
    )
    wound = total % LAT
    angle = -2.0 * np.pi / LAT * wound.astype(jnp.float32)
    return (jnp.cos(angle), jnp.sin(angle))


def apply_gamma(vectors):
    count = vectors.shape[1]
    sites = vectors.shape[3]
    shaped = vectors.reshape(2, count, 4, 3, sites)
    signs = jnp.array([-1.0, 1.0, 1.0, -1.0], jnp.float32)
    flipped = shaped[:, :, ::-1].astype(jnp.float32) * signs[None, None, :, None, None]
    return flipped.astype(jnp.bfloat16).reshape(2, count, 12, sites)


def phased_rows(wblock, cosine, sine):
    wreal = wblock[0].astype(jnp.float32)
    wimag = wblock[1].astype(jnp.float32)
    creal = cosine[:, None, None, :]
    cimag = sine[:, None, None, :]
    areal = wreal[None] * creal + wimag[None] * cimag
    aimag = wreal[None] * cimag - wimag[None] * creal
    rows = areal.shape[0] * areal.shape[1]
    width = areal.shape[2] * areal.shape[3]
    return jnp.concatenate([areal.reshape(rows, width), aimag.reshape(rows, width)], axis=0).astype(
        jnp.bfloat16
    )


def contract(lhs, block, nph, wrows):
    width = block.shape[2] * block.shape[3]
    rhs = jnp.concatenate([block[0].reshape(-1, width), block[1].reshape(-1, width)], axis=0)
    prod = lax.dot_general(lhs, rhs, (((1,), (1,)), ((), ())), preferred_element_type=jnp.float32)
    half_rows = nph * wrows
    half_cols = block.shape[1]
    real_part = prod[:half_rows, :half_cols] - prod[half_rows:, half_cols:]
    imag_part = prod[:half_rows, half_cols:] + prod[half_rows:, :half_cols]
    return jnp.stack([real_part, imag_part]).reshape(2, nph, wrows, half_cols)


def shards(w_modes, v_modes, momenta):
    wrows = w_modes.shape[1]
    sites = w_modes.shape[3]
    vrows = v_modes.shape[1]
    nph = momenta.shape[0]
    nmode = lax.axis_size("mode")
    reach = min(REACH, (nmode - 1) // 2)
    band_width = (2 * reach + 1) * vrows
    first = lax.axis_index("site") * sites
    cosine, sine = make_phase(momenta, first, sites)
    lhs = phased_rows(w_modes, cosine, sine)
    resident = apply_gamma(v_modes)
    accum = jnp.zeros((2, nph, wrows, band_width), jnp.float32)

    def handle(accum, block, offset):
        column = (offset + reach) * vrows
        part = contract(lhs, block, nph, wrows)
        return accum.at[:, :, :, column : column + vrows].set(part)

    moving = shifted(resident, "mode", reach)
    accum = handle(accum, moving, -reach)
    for step in range(1, 2 * reach + 1):
        moving = shifted(moving, "mode", -1)
        accum = handle(accum, moving, step - reach)
    return lax.psum_scatter(accum, "site", scatter_dimension=2, tiled=True)


def solution(mesh):
    placed = (P(None, ("grp", "mode"), None, "site"), P(None, ("grp", "mode"), None, "site"), P())
    return jax.shard_map(
        shards,
        mesh=mesh,
        in_specs=placed,
        out_specs=P(None, None, ("grp", "mode", "site"), None),
        check_vma=False,
    )
```

profile of v0, /device:TPU:0, one launch (start us, length us, event | category | flops | bytes accessed | tf_op | source)
XLA Modules:
  0.0 82.9 jit_solution(3586590455102904826)
XLA Ops:
  6.5 1.2 %multiply_convert_fusion = bf16[2,64,4,3,64]{4,1,3,2,0:T(8,128)(2,1)S(1)} fusion(f32[4]{0:T(128)} %constant.127.clone, bf16[2,64,4,3,64]{4,1,3,2,0:T(8,128)(2,1)} %bitcast.37), kind=kLoop, calls=%fused_computation.6 | loop fusion | flops 294912 | bytes 393232 | tf_op jit(solution)/shard_map/convert_element_type | solution.py:38
  7.7 3.1 %collective-permute-start = (bf16[2,64,12,64]{3,1,2,0:T(8,128)(2,1)S(1)}, bf16[2,64,12,64]{3,1,2,0:T(8,128)(2,1)S(1)}, u32[]{:S(2)}, u32[]{:S(2)}) collective-permute-start(bf16[2,64,12,64]{3,1,2,0:T(8,128)(2,1)S(1)} %bitcast.38), channel_id=1, source_target_pairs={{0,4},{4,8},{8,12},{12,0},{1,5},{5,9},{9,13},{13,1},{2,6},{6,10},{... | collective-permute-start | bytes 589832 | tf_op jit(solution)/shard_map/ppermute | solution.py:14
  10.8 1.0 %slice_reduce_fusion.2 = (s32[4]{0:T(128)S(1)}, s32[4]{0:T(128)S(1)}, s32[4]{0:T(128)S(1)}) fusion(s32[4,3]{1,0:T(4,128)} %param.12), kind=kLoop, calls=%fused_computation.35 | loop fusion | bytes 96 | tf_op jit(solution)/shard_map/slice | solution.py:23
  12.2 1.1 %bitcast_convert_fusion.1 = (f32[128,12,64]{0,2,1:T(8,128)S(1)}, f32[128,12,64]{0,2,1:T(8,128)S(1)}) fusion(bf16[2,128,12,64]{1,3,2,0:T(8,128)(2,1)} %param.10), kind=kLoop, calls=%fused_computation.22 | loop fusion | flops 196608 | bytes 1179648 | tf_op jit(solution)/shard_map/mul | solution.py:46
  13.3 0.9 %subtract_convert_fusion = (bf16[4,128,12,64]{1,0,3,2:T(4,128)(2,1)S(1)}, bf16[4,128,12,64]{1,0,3,2:T(4,128)(2,1)S(1)}) fusion(f32[4,64]{0,1:T(8,128)S(1)} %copy.33, f32[128,12,64]{0,2,1:T(8,128)S(1)} %get-tuple-element.59, f32[4,64]{0,1:T(8,128)S(1)} %copy.32, f32[128,12,64]{0,2,1:T(8,128)S(1)} %get-tuple-element.58), kind=kLoop, calls=%fused_computation | loop fusion | flops 3145728 | bytes 2361344 | tf_op jit(solution)/shard_map/convert.4
  14.2 0.1 bitcast_dynamic-update-slice_fusion.1
  14.4 0.1 bitcast_dynamic-update-slice_fusion
  14.5 7.4 %collective-permute-done = bf16[2,64,12,64]{3,1,2,0:T(8,128)(2,1)S(1)} collective-permute-done((bf16[2,64,12,64]{3,1,2,0:T(8,128)(2,1)S(1)}, bf16[2,64,12,64]{3,1,2,0:T(8,128)(2,1)S(1)}, u32[]{:S(2)}, u32[]{:S(2)}) %collective-permute-start) | collective-permute-done | bytes 196640 | tf_op jit(solution)/shard_map/ppermute | solution.py:14
  22.0 0.1 copy.34
  22.1 0.2 reshape_squeeze.18
  22.3 0.1 copy.35
  22.4 0.2 reshape_squeeze.19
  22.6 0.4 fusion
  23.0 1.8 %collective-permute-start.1 = (bf16[2,64,12,64]{3,1,2,0:T(8,128)(2,1)S(1)}, bf16[2,64,12,64]{3,1,2,0:T(8,128)(2,1)}, u32[]{:S(2)}, u32[]{:S(2)}) collective-permute-start(bf16[2,64,12,64]{3,1,2,0:T(8,128)(2,1)S(1)} %collective-permute-done), channel_id=1, source_target_pairs={{0,12},{4,0},{8,4},{12,8},{1,13},{5,1},{9,5},{13,9},{2,14},{6,2},{... | collective-permute-start | bytes 589832 | tf_op jit(solution)/shard_map/ppermute | solution.py:14
  25.2 8.3 %collective-permute-done.1 = bf16[2,64,12,64]{3,1,2,0:T(8,128)(2,1)} collective-permute-done((bf16[2,64,12,64]{3,1,2,0:T(8,128)(2,1)S(1)}, bf16[2,64,12,64]{3,1,2,0:T(8,128)(2,1)}, u32[]{:S(2)}, u32[]{:S(2)}) %collective-permute-start.1) | collective-permute-done | bytes 196640 | tf_op jit(solution)/shard_map/ppermute | solution.py:14
  33.4 1.0 %fusion.22 = (bf16[1,64,12,64]{3,1,2,0:T(8,128)(2,1)S(1)}, bf16[1,64,12,64]{3,1,2,0:T(8,128)(2,1)S(1)}) fusion(bf16[2,64,12,64]{3,1,2,0:T(8,128)(2,1)} %collective-permute-done.1), kind=kLoop, calls=%fused_computation.49 | loop fusion | bytes 393216 | tf_op jit(solution)/shard_map/slice | solution.py:57
  34.5 0.1 copy.38
  34.6 0.2 reshape_squeeze.20
  35.0 0.2 reshape_squeeze.21
  35.1 0.4 fusion.4
  35.5 3.3 %collective-permute-start.2 = (bf16[2,64,12,64]{3,1,2,0:T(8,128)(2,1)}, bf16[2,64,12,64]{3,1,2,0:T(8,128)(2,1)}, u32[]{:S(2)}, u32[]{:S(2)}) collective-permute-start(bf16[2,64,12,64]{3,1,2,0:T(8,128)(2,1)} %collective-permute-done.1), channel_id=1, source_target_pairs={{0,12},{4,0},{8,4},{12,8},{1,13},{5,1},{9,5},{13,9},{2,14},{6,2},{... | collective-permute-start | bytes 589832 | tf_op jit(solution)/shard_map/ppermute | solution.py:14
  38.9 0.8 %copy.49 = f32[512,64]{1,0:T(8,128)} copy(f32[512,64]{0,1:T(8,128)S(1)} %get-tuple-element.49) | data formatting | bytes 262144 | tf_op jit(solution)/shard_map/stack | solution.py:63
  39.8 1.0 %pad_maximum_fusion = f32[2,4,128,64]{3,2,1,0:T(8,128)S(1)} fusion(f32[1,4,128,64]{3,2,1,0:T(8,128)} %bitcast.36, f32[1,4,128,64]{3,2,1,0:T(8,128)S(1)} %bitcast.33), kind=kLoop, calls=%fused_computation.7 | loop fusion | flops 65536 | bytes 524288 | tf_op jit(solution)/shard_map/stack | solution.py:63
  40.8 3.1 %scatter.11 = f32[2,4,128,192]{3,2,1,0:T(8,128)S(1)} dynamic-update-slice(f32[2,4,128,192]{3,2,1,0:T(8,128)S(1)} %select_maximum_fusion, f32[2,4,128,64]{3,2,1,0:T(8,128)S(1)} %pad_maximum_fusion, s32[]{:T(128)} %constant.120.clone.1, s32[]{:T(128)} %constant.120.clone.1, s32[]{:T(128)} %constant.120.clone.1, s32[]{:T(128)} %constant.118.clone.1) | dynamic-update-slice | bytes 524292 | tf_op jit(solution)/shard_map/scatter | solution.py:83
  43.8 1.8 %collective-permute-done.2 = bf16[2,64,12,64]{3,1,2,0:T(8,128)(2,1)} collective-permute-done((bf16[2,64,12,64]{3,1,2,0:T(8,128)(2,1)}, bf16[2,64,12,64]{3,1,2,0:T(8,128)(2,1)}, u32[]{:S(2)}, u32[]{:S(2)}) %collective-permute-start.2) | collective-permute-done | bytes 196640 | tf_op jit(solution)/shard_map/ppermute | solution.py:14
  45.7 1.0 %fusion.21 = (bf16[1,64,12,64]{3,1,2,0:T(8,128)(2,1)S(1)}, bf16[1,64,12,64]{3,1,2,0:T(8,128)(2,1)S(1)}) fusion(bf16[2,64,12,64]{3,1,2,0:T(8,128)(2,1)} %collective-permute-done.2), kind=kLoop, calls=%fused_computation.48 | loop fusion | bytes 393216 | tf_op jit(solution)/shard_map/slice | solution.py:57
  46.7 0.1 copy.42
  46.9 0.2 reshape_squeeze.22
  47.2 0.2 reshape_squeeze.23
  47.4 0.4 fusion.8
  48.1 1.0 %copy-done = f32[2,4,128,192]{3,2,1,0:T(8,128)} copy-done((f32[2,4,128,192]{3,2,1,0:T(8,128)}, f32[2,4,128,192]{3,2,1,0:T(8,128)S(1)}, u32[]{:S(2)}) %copy-start) | copy-done | bytes 786456
  49.1 27.0 %reduce-scatter.2.cloned.1.call-done = f32[2,4,32,192]{3,2,1,0:T(8,128)} async-done(((f32[2,4,128,192]{3,2,1,0:T(8,128)}), f32[2,4,32,192]{3,2,1,0:T(8,128)}) %reduce-scatter.2.cloned.1.call-update) | async-done | bytes 196624 | tf_op jit(solution)/shard_map/reduce_scatter | solution.py:90
  (21 shorter events, 1.6 us)
Async XLA Ops:
  6.5 69.5 %reduce-scatter.2.cloned.1.call-start = ((), (), s32[]{:S(2)}) async-start(), calls=%async_computation.1 | async-start | bytes 1310720 | tf_op jit(solution)/shard_map/reduce_scatter | solution.py:90
  7.7 14.2 %collective-permute-start = (bf16[2,64,12,64]{3,1,2,0:T(8,128)(2,1)S(1)}, bf16[2,64,12,64]{3,1,2,0:T(8,128)(2,1)S(1)}, u32[]{:S(2)}, u32[]{:S(2)}) collective-permute-start(bf16[2,64,12,64]{3,1,2,0:T(8,128)(2,1)S(1)} %bitcast.38), channel_id=1, source_target_pairs={{0,4},{4,8},{8,12},{12,0},{1,5},{5,9},{9,13},{13,1},{2,6},{6,10},{... | collective-permute-start | bytes 589832 | tf_op jit(solution)/shard_map/ppermute | solution.py:14
  23.0 10.5 %collective-permute-start.1 = (bf16[2,64,12,64]{3,1,2,0:T(8,128)(2,1)S(1)}, bf16[2,64,12,64]{3,1,2,0:T(8,128)(2,1)}, u32[]{:S(2)}, u32[]{:S(2)}) collective-permute-start(bf16[2,64,12,64]{3,1,2,0:T(8,128)(2,1)S(1)} %collective-permute-done), channel_id=1, source_target_pairs={{0,12},{4,0},{8,4},{12,8},{1,13},{5,1},{9,5},{13,9},{2,14},{6,2},{... | collective-permute-start | bytes 589832 | tf_op jit(solution)/shard_map/ppermute | solution.py:14
  35.5 10.2 %collective-permute-start.2 = (bf16[2,64,12,64]{3,1,2,0:T(8,128)(2,1)}, bf16[2,64,12,64]{3,1,2,0:T(8,128)(2,1)}, u32[]{:S(2)}, u32[]{:S(2)}) collective-permute-start(bf16[2,64,12,64]{3,1,2,0:T(8,128)(2,1)} %collective-permute-done.1), channel_id=1, source_target_pairs={{0,12},{4,0},{8,4},{12,8},{1,13},{5,1},{9,5},{13,9},{2,14},{6,2},{... | collective-permute-start | bytes 589832 | tf_op jit(solution)/shard_map/ppermute | solution.py:14
  48.1 1.0 %copy-start = (f32[2,4,128,192]{3,2,1,0:T(8,128)}, f32[2,4,128,192]{3,2,1,0:T(8,128)S(1)}, u32[]{:S(2)}) copy-start(f32[2,4,128,192]{3,2,1,0:T(8,128)S(1)} %maximum_dynamic-update-slice_fusion) | copy-start | bytes 2359300
Sparse Core Ops, SparseCore 0:
  49.2 26.8 reduce-scatter.1
where the time goes:
time: 83.2 us; the launch traced here: 82.9 us
  waiting for transfers between devices  44.5 us (53%)
  between operations  13.6 us (16%)
  local copies, waits for them, and re-layouts  10.9 us (13%)
  starting transfers between devices  8.14 us (10%)
  other arithmetic  4.6 us (6%)
  matrix products  1.14 us (1%)
    reduce_scatter x1, waiting for transfers between devices, shards(): return lax.psum_scatter(accum, 'site', scatter_dimension=2, tiled=True)  27 us
    ppermute x3, waiting for transfers between devices, shifted(): return lax.ppermute(value, axis, pairs)  17.5 us
    ppermute x3, starting transfers between devices, shifted(): return lax.ppermute(value, axis, pairs)  8.14 us
    scatter x1, local copies, waits for them, and re-layouts, handle(): return accum.at[:, :, :, column:column + vrows].set(part)  3.05 us
    slice x6, local copies, waits for them, and re-layouts, contract(): block[0].reshape(-1, width)  2.54 us
  transfers between devices with their start and end apart: 4, of which 4 were waited for; matrix products, arithmetic and copies ran while one was open for 11% of the time, Pallas kernels for 0%

commit v1 on v0

v1 whole, which is shorter than its diff:
```python
import functools

import jax
import jax.numpy as jnp
import numpy as np
from jax import lax
from jax.experimental import pallas as pl
from jax.experimental.pallas import tpu as pltpu
from jax.sharding import PartitionSpec as P

LAT = 96
REACH = 4
SPINS = 4
SIGNS = (-1.0, 1.0, 1.0, -1.0)
MESH = pl.DeviceIdType.MESH


def phase_table(mom_ref, nph, rows, sites):
    shape = (sites, nph * rows)
    index = lax.axis_index("site") * sites + lax.broadcasted_iota(jnp.int32, shape, 0)
    lane = lax.broadcasted_iota(jnp.int32, shape, 1)
    lat = jnp.full(shape, LAT, jnp.int32)
    xcoord = lax.rem(index, lat)
    upper = lax.div(index, lat)
    ycoord = lax.rem(upper, lat)
    zcoord = lax.div(upper, lat)
    total = jnp.zeros(shape, jnp.int32)
    for p in range(nph):
        here = mom_ref[p, 0] * xcoord + mom_ref[p, 1] * ycoord + mom_ref[p, 2] * zcoord
        total = jnp.where((lane >= p * rows) & (lane < (p + 1) * rows), here, total)
    wound = lax.rem(total, lat)
    wound = jnp.where(wound < 0, wound + LAT, wound)
    angle = (-2.0 * np.pi / LAT) * wound.astype(jnp.float32)
    return jnp.cos(angle), jnp.sin(angle)


def kernel(
    nmode, nsite, reach,
    w_hbm, v_hbm, mom_ref, out_ref,
    w_ref, v_ref, packed, arrived, lhs, outgoing, incoming, total,
    load_sem, vsend_sem, vrecv_sem, psend_sem, precv_sem,
):
    mode = lax.axis_index("mode")
    site = lax.axis_index("site")
    _, nsc, sites, wrows = w_ref.shape
    nph = mom_ref.shape[0]
    rows = wrows // nsite
    half = nph * rows
    vrows = packed.shape[0]
    nblocks = 2 * reach + 1
    step = 1 - 2 * lax.rem(site, 2) if nsite % 2 == 0 else 1

    load_v = pltpu.make_async_copy(v_hbm, v_ref, load_sem.at[0])
    load_w = pltpu.make_async_copy(w_hbm, w_ref, load_sem.at[1])
    load_v.start()
    load_w.start()

    def mode_of(offset):
        return {"mode": lax.rem(mode + offset + nmode, nmode)}

    def site_of(distance):
        return lax.rem(site + step * distance + nsite, nsite)

    barrier = pltpu.get_barrier_semaphore()
    offsets = [o for o in range(-reach, reach + 1) if o != 0]
    for offset in offsets:
        pl.semaphore_signal(barrier, inc=1, device_id=mode_of(offset), device_id_type=MESH)
    for distance in range(1, nsite):
        pl.semaphore_signal(
            barrier, inc=1, device_id={"site": site_of(distance)}, device_id_type=MESH
        )

    load_v.wait()
    for sc in range(nsc):
        packed[:, sc * 2 * sites : (sc + 1) * 2 * sites] = jnp.concatenate(
            [v_ref[0, sc], v_ref[1, sc]], axis=1
        )
    pl.semaphore_wait(barrier, len(offsets) + nsite - 1)

    vcopies = []
    for far in range(1, reach + 1):
        for offset in (far, -far):
            slot = offset + reach
            copy = pltpu.make_async_remote_copy(
                src_ref=packed,
                dst_ref=arrived.at[slot],
                send_sem=vsend_sem.at[slot],
                recv_sem=vrecv_sem.at[slot],
                device_id=mode_of(-offset),
                device_id_type=MESH,
            )
            copy.start()
            vcopies.append(copy)

    cosine, sine = phase_table(mom_ref, nph, rows, sites)
    cosine = jnp.concatenate([cosine] * nsite, axis=1)
    sine = jnp.concatenate([sine] * nsite, axis=1)
    shape = (wrows, nsite * half)
    mode_row = lax.broadcasted_iota(jnp.int32, shape, 0)
    lane = lax.broadcasted_iota(jnp.int32, shape, 1)
    spread = jnp.zeros(shape, jnp.float32)
    for piece in range(nsite * nph):
        source = lane - piece * rows + (piece // nph) * rows
        inside = (lane >= piece * rows) & (lane < (piece + 1) * rows)
        spread = jnp.where(inside & (mode_row == source), 1.0, spread)
    spread = spread.astype(jnp.bfloat16)

    load_w.wait()
    colours = nsc // SPINS
    for sc in range(nsc):
        spin, colour = sc // colours, sc % colours
        sign = SIGNS[spin]
        source = colours * (SPINS - 1 - spin) + colour
        wreal = jnp.dot(w_ref[0, source], spread, preferred_element_type=jnp.float32)
        wimag = jnp.dot(w_ref[1, source], spread, preferred_element_type=jnp.float32)
        areal = (sign * (wreal * cosine + wimag * sine)).astype(jnp.bfloat16)
        aimag = (sign * (wreal * sine - wimag * cosine)).astype(jnp.bfloat16)
        top = pl.ds(sc * 2 * sites, sites)
        low = pl.ds(sc * 2 * sites + sites, sites)
        for s in range(nsite):
            part = slice(s * half, (s + 1) * half)
            lhs[s, top, 0:half] = areal[:, part]
            lhs[s, top, half : 2 * half] = aimag[:, part]
            lhs[s, low, 0:half] = -aimag[:, part]
            lhs[s, low, half : 2 * half] = areal[:, part]

    distances = list(range(nsite - 1, 0, -1))
    if nsite > 2:
        distances.remove(nsite // 2)
        distances.insert(0, nsite // 2)

    def partial_copy(slot, distance):
        return pltpu.make_async_remote_copy(
            src_ref=outgoing.at[slot, distance - 1],
            dst_ref=incoming.at[slot, distance - 1],
            send_sem=psend_sem.at[slot, distance - 1],
            recv_sem=precv_sem.at[slot, distance - 1],
            device_id={"site": site_of(distance)},
            device_id_type=MESH,
        )

    def handle(block, slot):
        for distance in distances:
            outgoing[slot, distance - 1] = jnp.dot(
                block, lhs[site_of(distance)], preferred_element_type=jnp.float32
            ).astype(jnp.bfloat16)
            partial_copy(slot, distance).start()
        total[slot] = jnp.dot(block, lhs[site], preferred_element_type=jnp.float32)

    handle(packed[...], reach)
    first = jnp.where(2 * mode < nmode, 1, -1)
    for far in range(1, reach + 1):
        for direction in (first, -first):
            slot = reach + direction * far
            pltpu.make_async_remote_copy(
                src_ref=packed,
                dst_ref=arrived.at[slot],
                send_sem=vsend_sem.at[slot],
                recv_sem=vrecv_sem.at[slot],
                device_id=mode_of(-1),
                device_id_type=MESH,
            ).wait_recv()
            handle(arrived[slot], slot)

    for slot in range(nblocks):
        value = total[slot]
        for distance in distances:
            partial_copy(slot, distance).wait_recv()
            value = value + incoming[slot, distance - 1].astype(jnp.float32)
        out_ref[:, slot * vrows : (slot + 1) * vrows] = value.T
    for copy in vcopies:
        copy.wait_send()
    for slot in range(nblocks):
        for distance in distances:
            partial_copy(slot, distance).wait_send()


def shards(nmode, nsite, w_modes, v_modes, momenta):
    _, wrows, nsc, sites = w_modes.shape
    vrows = v_modes.shape[1]
    nph = momenta.shape[0]
    reach = min(REACH, (nmode - 1) // 2)
    nblocks = 2 * reach + 1
    rows = wrows // nsite
    width = 2 * nsc * sites
    lanes = 2 * nph * rows
    out = pl.pallas_call(
        functools.partial(kernel, nmode, nsite, reach),
        out_shape=jax.ShapeDtypeStruct((lanes, nblocks * vrows), jnp.float32),
        in_specs=[
            pl.BlockSpec(memory_space=pl.ANY),
            pl.BlockSpec(memory_space=pl.ANY),
            pl.BlockSpec(memory_space=pltpu.SMEM),
        ],
        out_specs=pl.BlockSpec(memory_space=pltpu.VMEM),
        scratch_shapes=[
            pltpu.VMEM((2, nsc, sites, wrows), jnp.bfloat16),
            pltpu.VMEM((2, nsc, vrows, sites), jnp.bfloat16),
            pltpu.VMEM((vrows, width), jnp.bfloat16),
            pltpu.VMEM((nblocks, vrows, width), jnp.bfloat16),
            pltpu.VMEM((nsite, width, lanes), jnp.bfloat16),
            pltpu.VMEM((nblocks, nsite - 1, vrows, lanes), jnp.bfloat16),
            pltpu.VMEM((nblocks, nsite - 1, vrows, lanes), jnp.bfloat16),
            pltpu.VMEM((nblocks, vrows, lanes), jnp.float32),
            pltpu.SemaphoreType.DMA((2,)),
            pltpu.SemaphoreType.DMA((nblocks,)),
            pltpu.SemaphoreType.DMA((nblocks,)),
            pltpu.SemaphoreType.DMA((nblocks, nsite - 1)),
            pltpu.SemaphoreType.DMA((nblocks, nsite - 1)),
        ],
        compiler_params=pltpu.CompilerParams(
            collective_id=0, has_side_effects=True, vmem_limit_bytes=40 * 1024 * 1024
        ),
    )(jnp.transpose(w_modes, (0, 2, 3, 1)), jnp.transpose(v_modes, (0, 2, 1, 3)), momenta)
    return out.reshape(2, nph, rows, nblocks * vrows)


def solution(mesh):
    placed = (P(None, ("grp", "mode"), None, "site"), P(None, ("grp", "mode"), None, "site"), P())
    return jax.shard_map(
        functools.partial(shards, mesh.shape["mode"], mesh.shape["site"]),
        mesh=mesh,
        in_specs=placed,
        out_specs=P(None, None, ("grp", "mode", "site"), None),
        check_vma=False,
    )
```

time: 83.2 us -> 24 us (0.29)
  waiting for transfers between devices: 44.5 us -> 0 us
  Pallas kernels: 0 us -> 20.4 us
  between operations: 13.6 us -> 0.01 us
  starting transfers between devices: 8.14 us -> 0 us
  local copies, waits for them, and re-layouts: 10.9 us -> 3.38 us
  other arithmetic: 4.6 us -> 0 us
  matrix products: 1.14 us -> 0 us
    reduce_scatter x1 -> x0, waiting for transfers between devices: 27 us -> none  [shards(): return lax.psum_scatter(accum, 'site', scatter_dimension=2, tiled=True)]
    pallas_call x0 -> x1, Pallas kernels: none -> 20.4 us  [shards(): pl.pallas_call(functools.partial(kernel, nmode, nsite, reach), out_shape=...]
    ppermute x3 -> x0, waiting for transfers between devices: 17.5 us -> none  [shifted(): return lax.ppermute(value, axis, pairs)]
    ppermute x3 -> x0, starting transfers between devices: 8.14 us -> none  [shifted(): return lax.ppermute(value, axis, pairs)]
    slice x10 -> x0, local copies, waits for them, and re-layouts: 3.96 us -> none  [the longest x6 2.54 us: contract(): block[0].reshape(-1, width)]
    scatter x1 -> x0, local copies, waits for them, and re-layouts: 3.05 us -> none  [handle(): return accum.at[:, :, :, column:column + vrows].set(part)]
    another operation x12 -> x0, local copies, waits for them, and re-layouts: 2.46 us -> none  [the longest x6 1.46 us: contract(): return jnp.stack([real_part, imag_part]).reshape(2, nph, wrows, half_cols)]
    unnamed x3 -> x7, local copies, waits for them, and re-layouts: 1.11 us -> 3.38 us
  transfers between devices with their start and end apart: 4 -> 0, of which waited for: 4 -> 0; matrix products, arithmetic and copies ran while one was open for 11% -> 0% of each run, Pallas kernels for 0% -> 0%
where the time goes in v1:
time: 24 us; the launch traced here: 23.8 us
  Pallas kernels  20.4 us (85%)
  local copies, waits for them, and re-layouts  3.38 us (14%)
    pallas_call x1, Pallas kernels, shards(): pl.pallas_call(functools.partial(kernel, nmode, nsite, reach), out_shape=...  20.4 us
    unnamed x7, local copies, waits for them, and re-layouts  3.38 us

profile of v1, /device:TPU:0, one launch (start us, length us, event | category | flops | bytes accessed | tf_op | source)
XLA Modules:
  0.0 23.8 jit_solution(16197049049956710415)
XLA Ops:
  0.0 0.0 copy-start.2
  0.0 0.7 %copy-done.2 = s32[4,3]{1,0:T(4,128)S(1)} copy-done((s32[4,3]{1,0:T(4,128)S(1)}, s32[4,3]{1,0:T(4,128)}, u32[]{:S(2)}) %copy-start.2) | copy-done | bytes 72
  0.7 0.0 copy-start
  0.7 1.0 %copy-done = bf16[2,128,12,64]{1,3,2,0:T(8,128)(2,1)S(1)} copy-done((bf16[2,128,12,64]{1,3,2,0:T(8,128)(2,1)S(1)}, bf16[2,128,12,64]{1,3,2,0:T(8,128)(2,1)}, u32[]{:S(2)}) %copy-start) | copy-done | bytes 393240
  1.7 0.0 copy-start.1
  1.7 1.0 %copy-done.1 = bf16[2,64,12,64]{3,1,2,0:T(8,128)(2,1)S(1)} copy-done((bf16[2,64,12,64]{3,1,2,0:T(8,128)(2,1)S(1)}, bf16[2,64,12,64]{3,1,2,0:T(8,128)(2,1)}, u32[]{:S(2)}) %copy-start.1) | copy-done | bytes 196632
  2.7 20.4 %shard_map.37 = f32[256,192]{1,0:T(8,128)S(1)} custom-call(bf16[2,12,64,128]{3,2,1,0:T(8,128)(2,1)S(1)} %bitcast.4, bf16[2,12,64,64]{3,2,1,0:T(8,128)(2,1)S(1)} %bitcast.5, s32[4,3]{1,0:T(4,128)S(1)} %copy-done.2), custom_call_target="tpu_custom_call" | custom-call | tf_op jit(solution)/shard_map/pallas_call | solution.py:187
  23.1 0.7 %copy.5 = f32[2,4,32,192]{3,2,1,0:T(8,128)} copy(f32[2,4,32,192]{3,2,1,0:T(8,128)S(1)} %bitcast.3) | data formatting | bytes 393216
Async XLA Ops:
  0.0 0.7 %copy-start.2 = (s32[4,3]{1,0:T(4,128)S(1)}, s32[4,3]{1,0:T(4,128)}, u32[]{:S(2)}) copy-start(s32[4,3]{1,0:T(4,128)} %mom_ref.1) | copy-start | bytes 148
  0.7 1.0 %copy-start = (bf16[2,128,12,64]{1,3,2,0:T(8,128)(2,1)S(1)}, bf16[2,128,12,64]{1,3,2,0:T(8,128)(2,1)}, u32[]{:S(2)}) copy-start(bf16[2,128,12,64]{1,3,2,0:T(8,128)(2,1)} %param.3) | copy-start | bytes 1179652
  1.7 1.0 %copy-start.1 = (bf16[2,64,12,64]{3,1,2,0:T(8,128)(2,1)S(1)}, bf16[2,64,12,64]{3,1,2,0:T(8,128)(2,1)}, u32[]{:S(2)}) copy-start(bf16[2,64,12,64]{3,1,2,0:T(8,128)(2,1)} %param.4) | copy-start | bytes 589828

commit v2 on v1

--- a/solution.py
+++ b/solution.py
@@ -11,6 +11,7 @@
 LAT = 96
 REACH = 4
 SPINS = 4
+PIECES = 2
 SIGNS = (-1.0, 1.0, 1.0, -1.0)
 MESH = pl.DeviceIdType.MESH
 
@@ -36,8 +37,8 @@
 
 def kernel(
     nmode, nsite, reach,
-    w_hbm, v_hbm, mom_ref, out_ref,
-    w_ref, v_ref, packed, arrived, lhs, outgoing, incoming, total,
+    w_hbm, v_hbm, mom_hbm, out_ref,
+    w_ref, v_ref, mom_ref, packed, arrived, lhs, outgoing, incoming, total,
     load_sem, vsend_sem, vrecv_sem, psend_sem, precv_sem,
 ):
     mode = lax.axis_index("mode")
@@ -46,13 +47,16 @@
     nph = mom_ref.shape[0]
     rows = wrows // nsite
     half = nph * rows
-    vrows = packed.shape[0]
+    npiece, prows, _ = packed.shape
+    vrows = npiece * prows
     nblocks = 2 * reach + 1
     step = 1 - 2 * lax.rem(site, 2) if nsite % 2 == 0 else 1
 
     load_v = pltpu.make_async_copy(v_hbm, v_ref, load_sem.at[0])
     load_w = pltpu.make_async_copy(w_hbm, w_ref, load_sem.at[1])
+    load_mom = pltpu.make_async_copy(mom_hbm, mom_ref, load_sem.at[2])
     load_v.start()
+    load_mom.start()
     load_w.start()
 
     def mode_of(offset):
@@ -71,27 +75,33 @@
         )
 
     load_v.wait()
-    for sc in range(nsc):
-        packed[:, sc * 2 * sites : (sc + 1) * 2 * sites] = jnp.concatenate(
-            [v_ref[0, sc], v_ref[1, sc]], axis=1
+    for piece in range(npiece):
+        taken = slice(piece * prows, (piece + 1) * prows)
+        for sc in range(nsc):
+            packed[piece, :, sc * 2 * sites : (sc + 1) * 2 * sites] = jnp.concatenate(
+                [v_ref[0, sc, taken], v_ref[1, sc, taken]], axis=1
+            )
+    pl.semaphore_wait(barrier, len(offsets) + nsite - 1)
+
+    def vcopy(offset, piece):
+        slot = offset + reach
+        return pltpu.make_async_remote_copy(
+            src_ref=packed.at[piece],
+            dst_ref=arrived.at[slot, piece],
+            send_sem=vsend_sem.at[slot, piece],
+            recv_sem=vrecv_sem.at[slot, piece],
+            device_id=mode_of(-offset),
+            device_id_type=MESH,
         )
-    pl.semaphore_wait(barrier, len(offsets) + nsite - 1)
-
-    vcopies = []
-    for far in range(1, reach + 1):
-        for offset in (far, -far):
-            slot = offset + reach
-            copy = pltpu.make_async_remote_copy(
-                src_ref=packed,
-                dst_ref=arrived.at[slot],
-                send_sem=vsend_sem.at[slot],
-                recv_sem=vrecv_sem.at[slot],
-                device_id=mode_of(-offset),
-                device_id_type=MESH,
-            )
-            copy.start()
-            vcopies.append(copy)
-
+
+    toward = jnp.where(2 * mode < nmode, 1, -1)
+    order = [toward * far for far in range(1, reach + 1)]
+    order = [side * offset for offset in order for side in (1, -1)]
+    for offset in order:
+        for piece in range(npiece):
+            vcopy(offset, piece).start()
+
+    load_mom.wait()
     cosine, sine = phase_table(mom_ref, nph, rows, sites)
     cosine = jnp.concatenate([cosine] * nsite, axis=1)
     sine = jnp.concatenate([sine] * nsite, axis=1)
@@ -129,50 +139,46 @@
         distances.remove(nsite // 2)
         distances.insert(0, nsite // 2)
 
-    def partial_copy(slot, distance):
+    def partial_copy(slot, piece, distance):
         return pltpu.make_async_remote_copy(
-            src_ref=outgoing.at[slot, distance - 1],
-            dst_ref=incoming.at[slot, distance - 1],
-            send_sem=psend_sem.at[slot, distance - 1],
-            recv_sem=precv_sem.at[slot, distance - 1],
+            src_ref=outgoing.at[slot, piece, distance - 1],
+            dst_ref=incoming.at[slot, piece, distance - 1],
+            send_sem=psend_sem.at[slot, piece, distance - 1],
+            recv_sem=precv_sem.at[slot, piece, distance - 1],
             device_id={"site": site_of(distance)},
             device_id_type=MESH,
         )
 
-    def handle(block, slot):
+    def handle(block, slot, piece):
         for distance in distances:
-            outgoing[slot, distance - 1] = jnp.dot(
+            outgoing[slot, piece, distance - 1] = jnp.dot(
                 block, lhs[site_of(distance)], preferred_element_type=jnp.float32
             ).astype(jnp.bfloat16)
-            partial_copy(slot, distance).start()
-        total[slot] = jnp.dot(block, lhs[site], preferred_element_type=jnp.float32)
-
-    handle(packed[...], reach)
-    first = jnp.where(2 * mode < nmode, 1, -1)
-    for far in range(1, reach + 1):
-        for direction in (first, -first):
-            slot = reach + direction * far
-            pltpu.make_async_remote_copy(
-                src_ref=packed,
-                dst_ref=arrived.at[slot],
-                send_sem=vsend_sem.at[slot],
-                recv_sem=vrecv_sem.at[slot],
-                device_id=mode_of(-1),
-                device_id_type=MESH,
-            ).wait_recv()
-            handle(arrived[slot], slot)
+            partial_copy(slot, piece, distance).start()
+        total[slot, piece] = jnp.dot(block, lhs[site], preferred_element_type=jnp.float32)
+
+    for piece in range(npiece):
+        handle(packed[piece], reach, piece)
+    for offset in order:
+        for piece in range(npiece):
+            vcopy(offset, piece).wait_recv()
+            handle(arrived[offset + reach, piece], offset + reach, piece)
 
     for slot in range(nblocks):
-        value = total[slot]
-        for distance in distances:
-            partial_copy(slot, distance).wait_recv()
-            value = value + incoming[slot, distance - 1].astype(jnp.float32)
-        out_ref[:, slot * vrows : (slot + 1) * vrows] = value.T
-    for copy in vcopies:
-        copy.wait_send()
+        for piece in range(npiece):
+            value = total[slot, piece]
+            for distance in distances:
+                partial_copy(slot, piece, distance).wait_recv()
+                value = value + incoming[slot, piece, distance - 1].astype(jnp.float32)
+            total[slot, piece] = value
+    out_ref[...] = total[...].reshape(nblocks * vrows, 2 * half).T
+    for offset in order:
+        for piece in range(npiece):
+            vcopy(offset, piece).wait_send()
     for slot in range(nblocks):
-        for distance in distances:
-            partial_copy(slot, distance).wait_send()
+        for piece in range(npiece):
+            for distance in distances:
+                partial_copy(slot, piece, distance).wait_send()
 
 
 def shards(nmode, nsite, w_modes, v_modes, momenta):
@@ -184,32 +190,34 @@
     rows = wrows // nsite
     width = 2 * nsc * sites
     lanes = 2 * nph * rows
+    prows = vrows // PIECES
     out = pl.pallas_call(
         functools.partial(kernel, nmode, nsite, reach),
         out_shape=jax.ShapeDtypeStruct((lanes, nblocks * vrows), jnp.float32),
         in_specs=[
             pl.BlockSpec(memory_space=pl.ANY),
             pl.BlockSpec(memory_space=pl.ANY),
-            pl.BlockSpec(memory_space=pltpu.SMEM),
+            pl.BlockSpec(memory_space=pl.ANY),
         ],
         out_specs=pl.BlockSpec(memory_space=pltpu.VMEM),
         scratch_shapes=[
             pltpu.VMEM((2, nsc, sites, wrows), jnp.bfloat16),
             pltpu.VMEM((2, nsc, vrows, sites), jnp.bfloat16),
-            pltpu.VMEM((vrows, width), jnp.bfloat16),
-            pltpu.VMEM((nblocks, vrows, width), jnp.bfloat16),
+            pltpu.SMEM((nph, 3), jnp.int32),
+            pltpu.VMEM((PIECES, prows, width), jnp.bfloat16),
+            pltpu.VMEM((nblocks, PIECES, prows, width), jnp.bfloat16),
             pltpu.VMEM((nsite, width, lanes), jnp.bfloat16),
-            pltpu.VMEM((nblocks, nsite - 1, vrows, lanes), jnp.bfloat16),
-            pltpu.VMEM((nblocks, nsite - 1, vrows, lanes), jnp.bfloat16),
-            pltpu.VMEM((nblocks, vrows, lanes), jnp.float32),
-            pltpu.SemaphoreType.DMA((2,)),
-            pltpu.SemaphoreType.DMA((nblocks,)),
-            pltpu.SemaphoreType.DMA((nblocks,)),
-            pltpu.SemaphoreType.DMA((nblocks, nsite - 1)),
-            pltpu.SemaphoreType.DMA((nblocks, nsite - 1)),
+            pltpu.VMEM((nblocks, PIECES, nsite - 1, prows, lanes), jnp.bfloat16),
+            pltpu.VMEM((nblocks, PIECES, nsite - 1, prows, lanes), jnp.bfloat16),
+            pltpu.VMEM((nblocks, PIECES, prows, lanes), jnp.float32),
+            pltpu.SemaphoreType.DMA((3,)),
+            pltpu.SemaphoreType.DMA((nblocks, PIECES)),
+            pltpu.SemaphoreType.DMA((nblocks, PIECES)),
+            pltpu.SemaphoreType.DMA((nblocks, PIECES, nsite - 1)),
+            pltpu.SemaphoreType.DMA((nblocks, PIECES, nsite - 1)),
         ],
         compiler_params=pltpu.CompilerParams(
-            collective_id=0, has_side_effects=True, vmem_limit_bytes=40 * 1024 * 1024
+            collective_id=0, has_side_effects=True, vmem_limit_bytes=60 * 1024 * 1024
         ),
     )(jnp.transpose(w_modes, (0, 2, 3, 1)), jnp.transpose(v_modes, (0, 2, 1, 3)), momenta)
     return out.reshape(2, nph, rows, nblocks * vrows)

time: 24 us -> 23 us (0.958)
  local copies, waits for them, and re-layouts: 3.38 us -> 1.67 us
  Pallas kernels: 20.4 us -> 21.2 us
    unnamed x7 -> x1, local copies, waits for them, and re-layouts: 3.38 us -> 1.67 us
    pallas_call x1, Pallas kernels: 20.4 us -> 21.2 us  [shards(): pl.pallas_call(functools.partial(kernel, nmode, nsite, reach), out_shape=...]
where the time goes in v2:
time: 23 us; the launch traced here: 22.8 us
  Pallas kernels  21.2 us (92%)
  local copies, waits for them, and re-layouts  1.67 us (7%)
    pallas_call x1, Pallas kernels, shards(): pl.pallas_call(functools.partial(kernel, nmode, nsite, reach), out_shape=...  21.2 us
    unnamed x1, local copies, waits for them, and re-layouts  1.67 us

profile of v2, /device:TPU:0, one launch (start us, length us, event | category | flops | bytes accessed | tf_op | source)
XLA Modules:
  0.0 22.8 jit_solution(10242705948964815784)
XLA Ops:
  0.0 21.2 %shard_map.37 = f32[256,192]{1,0:T(8,128)} custom-call(bf16[2,12,64,128]{3,2,1,0:T(8,128)(2,1)} %bitcast.4, bf16[2,12,64,64]{3,2,1,0:T(8,128)(2,1)} %bitcast.5, s32[4,3]{1,0:T(4,128)} %mom_hbm.1), custom_call_target="tpu_custom_call" | custom-call | tf_op jit(solution)/shard_map/pallas_call | solution.py:194
  21.2 1.7 %copy.5 = f32[2,4,32,192]{3,2,1,0:T(8,128)} copy(f32[2,4,32,192]{3,2,1,0:T(8,128)} %bitcast.3) | data formatting | bytes 393216

commit v3 on v2

--- a/solution.py
+++ b/solution.py
@@ -52,10 +52,15 @@
     nblocks = 2 * reach + 1
     step = 1 - 2 * lax.rem(site, 2) if nsite % 2 == 0 else 1
 
-    load_v = pltpu.make_async_copy(v_hbm, v_ref, load_sem.at[0])
-    load_w = pltpu.make_async_copy(w_hbm, w_ref, load_sem.at[1])
-    load_mom = pltpu.make_async_copy(mom_hbm, mom_ref, load_sem.at[2])
-    load_v.start()
+    def load_v(piece):
+        return pltpu.make_async_copy(
+            v_hbm.at[:, :, pl.ds(piece * prows, prows), :], v_ref.at[piece], load_sem.at[2 + piece]
+        )
+
+    for piece in range(npiece):
+        load_v(piece).start()
+    load_w = pltpu.make_async_copy(w_hbm, w_ref, load_sem.at[0])
+    load_mom = pltpu.make_async_copy(mom_hbm, mom_ref, load_sem.at[1])
     load_mom.start()
     load_w.start()
 
@@ -73,15 +78,6 @@
         pl.semaphore_signal(
             barrier, inc=1, device_id={"site": site_of(distance)}, device_id_type=MESH
         )
-
-    load_v.wait()
-    for piece in range(npiece):
-        taken = slice(piece * prows, (piece + 1) * prows)
-        for sc in range(nsc):
-            packed[piece, :, sc * 2 * sites : (sc + 1) * 2 * sites] = jnp.concatenate(
-                [v_ref[0, sc, taken], v_ref[1, sc, taken]], axis=1
-            )
-    pl.semaphore_wait(barrier, len(offsets) + nsite - 1)
 
     def vcopy(offset, piece):
         slot = offset + reach
@@ -97,7 +93,16 @@
     toward = jnp.where(2 * mode < nmode, 1, -1)
     order = [toward * far for far in range(1, reach + 1)]
     order = [side * offset for offset in order for side in (1, -1)]
-    for offset in order:
+    for piece in range(npiece):
+        load_v(piece).wait()
+        for sc in range(nsc):
+            packed[piece, :, sc * 2 * sites : (sc + 1) * 2 * sites] = jnp.concatenate(
+                [v_ref[piece, 0, sc], v_ref[piece, 1, sc]], axis=1
+            )
+        if piece == 0:
+            pl.semaphore_wait(barrier, len(offsets) + nsite - 1)
+        vcopy(order[0], piece).start()
+    for offset in order[1:]:
         for piece in range(npiece):
             vcopy(offset, piece).start()
 
@@ -195,14 +200,14 @@
         functools.partial(kernel, nmode, nsite, reach),
         out_shape=jax.ShapeDtypeStruct((lanes, nblocks * vrows), jnp.float32),
         in_specs=[
-            pl.BlockSpec(memory_space=pl.ANY),
-            pl.BlockSpec(memory_space=pl.ANY),
-            pl.BlockSpec(memory_space=pl.ANY),
+            pl.BlockSpec(memory_space=pltpu.HBM),
+            pl.BlockSpec(memory_space=pltpu.HBM),
+            pl.BlockSpec(memory_space=pltpu.HBM),
         ],
         out_specs=pl.BlockSpec(memory_space=pltpu.VMEM),
         scratch_shapes=[
             pltpu.VMEM((2, nsc, sites, wrows), jnp.bfloat16),
-            pltpu.VMEM((2, nsc, vrows, sites), jnp.bfloat16),
+            pltpu.VMEM((PIECES, 2, nsc, prows, sites), jnp.bfloat16),
             pltpu.SMEM((nph, 3), jnp.int32),
             pltpu.VMEM((PIECES, prows, width), jnp.bfloat16),
             pltpu.VMEM((nblocks, PIECES, prows, width), jnp.bfloat16),
@@ -210,16 +215,20 @@
             pltpu.VMEM((nblocks, PIECES, nsite - 1, prows, lanes), jnp.bfloat16),
             pltpu.VMEM((nblocks, PIECES, nsite - 1, prows, lanes), jnp.bfloat16),
             pltpu.VMEM((nblocks, PIECES, prows, lanes), jnp.float32),
-            pltpu.SemaphoreType.DMA((3,)),
+            pltpu.SemaphoreType.DMA((2 + PIECES,)),
             pltpu.SemaphoreType.DMA((nblocks, PIECES)),
             pltpu.SemaphoreType.DMA((nblocks, PIECES)),
             pltpu.SemaphoreType.DMA((nblocks, PIECES, nsite - 1)),
             pltpu.SemaphoreType.DMA((nblocks, PIECES, nsite - 1)),
         ],
         compiler_params=pltpu.CompilerParams(
-            collective_id=0, has_side_effects=True, vmem_limit_bytes=60 * 1024 * 1024
+            collective_id=0, has_side_effects=True, vmem_limit_bytes=32 * 1024 * 1024
         ),
-    )(jnp.transpose(w_modes, (0, 2, 3, 1)), jnp.transpose(v_modes, (0, 2, 1, 3)), momenta)
+    )(
+        pltpu.with_memory_space_constraint(jnp.transpose(w_modes, (0, 2, 3, 1)), pltpu.HBM),
+        pltpu.with_memory_space_constraint(jnp.transpose(v_modes, (0, 2, 1, 3)), pltpu.HBM),
+        pltpu.with_memory_space_constraint(momenta, pltpu.HBM),
+    )
     return out.reshape(2, nph, rows, nblocks * vrows)
 
 

time: 23 us -> 21.3 us (0.926)
  local copies, waits for them, and re-layouts: 1.67 us -> 0.71 us
  Pallas kernels: 21.2 us -> 20.5 us
    unnamed x1, local copies, waits for them, and re-layouts: 1.67 us -> 0.71 us
    pallas_call x1, Pallas kernels: 21.2 us -> 20.5 us  [shards(): pl.pallas_call(functools.partial(kernel, nmode, nsite, reach), out_shape=...]
where the time goes in v3:
time: 21.3 us; the launch traced here: 21.2 us
  Pallas kernels  20.5 us (96%)
  local copies, waits for them, and re-layouts  0.71 us (3%)
    pallas_call x1, Pallas kernels, shards(): pl.pallas_call(functools.partial(kernel, nmode, nsite, reach), out_shape=...  20.5 us
    unnamed x1, local copies, waits for them, and re-layouts  0.71 us

profile of v3, /device:TPU:0, one launch (start us, length us, event | category | flops | bytes accessed | tf_op | source)
XLA Modules:
  0.0 21.2 jit_solution(9757805702534790952)
XLA Ops:
  0.0 20.5 %shard_map.37 = f32[256,192]{1,0:T(8,128)S(1)} custom-call(bf16[2,12,64,128]{3,2,1,0:T(8,128)(2,1)} %bitcast.4, bf16[2,12,64,64]{3,2,1,0:T(8,128)(2,1)} %bitcast.5, s32[4,3]{1,0:T(4,128)} %mom_hbm.1), custom_call_target="tpu_custom_call" | custom-call | tf_op jit(solution)/shard_map/pallas_call | solution.py:199
  20.5 0.7 %copy.5 = f32[2,4,32,192]{3,2,1,0:T(8,128)} copy(f32[2,4,32,192]{3,2,1,0:T(8,128)S(1)} %bitcast.3) | data formatting | bytes 393216

commit v4 on v3

--- a/solution.py
+++ b/solution.py
@@ -38,7 +38,8 @@
 def kernel(
     nmode, nsite, reach,
     w_hbm, v_hbm, mom_hbm, out_ref,
-    w_ref, v_ref, mom_ref, packed, arrived, lhs, outgoing, incoming, total,
+    w_ref, v_ref, mom_ref, packed, arrived, lhs, total,
+    own_out, band_out, own_in, band_in,
     load_sem, vsend_sem, vrecv_sem, psend_sem, precv_sem,
 ):
     mode = lax.axis_index("mode")
@@ -49,7 +50,8 @@
     half = nph * rows
     npiece, prows, _ = packed.shape
     vrows = npiece * prows
-    nblocks = 2 * reach + 1
+    outgoing = [own_out] + [band_out.at[piece] for piece in range(npiece)]
+    incoming = [own_in] + [band_in.at[piece] for piece in range(npiece)]
     step = 1 - 2 * lax.rem(site, 2) if nsite % 2 == 0 else 1
 
     def load_v(piece):
@@ -79,20 +81,16 @@
             barrier, inc=1, device_id={"site": site_of(distance)}, device_id_type=MESH
         )
 
-    def vcopy(offset, piece):
-        slot = offset + reach
+    def vcopy(piece, index):
         return pltpu.make_async_remote_copy(
             src_ref=packed.at[piece],
-            dst_ref=arrived.at[slot, piece],
-            send_sem=vsend_sem.at[slot, piece],
-            recv_sem=vrecv_sem.at[slot, piece],
-            device_id=mode_of(-offset),
+            dst_ref=arrived.at[piece, index],
+            send_sem=vsend_sem.at[piece, index],
+            recv_sem=vrecv_sem.at[piece, index],
+            device_id=mode_of(-offsets[index]),
             device_id_type=MESH,
         )
 
-    toward = jnp.where(2 * mode < nmode, 1, -1)
-    order = [toward * far for far in range(1, reach + 1)]
-    order = [side * offset for offset in order for side in (1, -1)]
     for piece in range(npiece):
         load_v(piece).wait()
         for sc in range(nsc):
@@ -101,10 +99,8 @@
             )
         if piece == 0:
             pl.semaphore_wait(barrier, len(offsets) + nsite - 1)
-        vcopy(order[0], piece).start()
-    for offset in order[1:]:
-        for piece in range(npiece):
-            vcopy(offset, piece).start()
+            for index in range(len(offsets)):
+                vcopy(piece, index).start()
 
     load_mom.wait()
     cosine, sine = phase_table(mom_ref, nph, rows, sites)
@@ -144,46 +140,64 @@
         distances.remove(nsite // 2)
         distances.insert(0, nsite // 2)
 
-    def partial_copy(slot, piece, distance):
+    def partial_copy(group, distance):
         return pltpu.make_async_remote_copy(
-            src_ref=outgoing.at[slot, piece, distance - 1],
-            dst_ref=incoming.at[slot, piece, distance - 1],
-            send_sem=psend_sem.at[slot, piece, distance - 1],
-            recv_sem=precv_sem.at[slot, piece, distance - 1],
+            src_ref=outgoing[group].at[distance - 1],
+            dst_ref=incoming[group].at[distance - 1],
+            send_sem=psend_sem.at[group, distance - 1],
+            recv_sem=precv_sem.at[group, distance - 1],
             device_id={"site": site_of(distance)},
             device_id_type=MESH,
         )
 
-    def handle(block, slot, piece):
+    def handle(group, block):
         for distance in distances:
-            outgoing[slot, piece, distance - 1] = jnp.dot(
+            outgoing[group][distance - 1] = jnp.dot(
                 block, lhs[site_of(distance)], preferred_element_type=jnp.float32
             ).astype(jnp.bfloat16)
-            partial_copy(slot, piece, distance).start()
-        total[slot, piece] = jnp.dot(block, lhs[site], preferred_element_type=jnp.float32)
-
+            partial_copy(group, distance).start()
+        own = jnp.dot(block, lhs[site], preferred_element_type=jnp.float32)
+        for start, stop, column in places(group):
+            total[column : column + stop - start, :] = own[start:stop]
+
+    def places(group):
+        if group == 0:
+            return [(0, vrows, reach * vrows)]
+        return [
+            (i * prows, (i + 1) * prows, (o + reach) * vrows + (group - 1) * prows)
+            for i, o in enumerate(offsets)
+        ]
+
+    def gather(group):
+        for distance in distances:
+            partial_copy(group, distance).wait_recv()
+        for start, stop, column in places(group):
+            value = total[column : column + stop - start, :]
+            for distance in distances:
+                value = value + incoming[group][distance - 1, start:stop].astype(jnp.float32)
+            total[column : column + stop - start, :] = value
+
+    def next_pieces(piece):
+        for index in range(len(offsets)):
+            vcopy(piece - 1, index).wait_send()
+            vcopy(piece, index).start()
+
+    next_pieces(1)
+    handle(0, packed[...].reshape(vrows, -1))
     for piece in range(npiece):
-        handle(packed[piece], reach, piece)
-    for offset in order:
-        for piece in range(npiece):
-            vcopy(offset, piece).wait_recv()
-            handle(arrived[offset + reach, piece], offset + reach, piece)
-
-    for slot in range(nblocks):
-        for piece in range(npiece):
-            value = total[slot, piece]
-            for distance in distances:
-                partial_copy(slot, piece, distance).wait_recv()
-                value = value + incoming[slot, piece, distance - 1].astype(jnp.float32)
-            total[slot, piece] = value
-    out_ref[...] = total[...].reshape(nblocks * vrows, 2 * half).T
-    for offset in order:
-        for piece in range(npiece):
-            vcopy(offset, piece).wait_send()
-    for slot in range(nblocks):
-        for piece in range(npiece):
-            for distance in distances:
-                partial_copy(slot, piece, distance).wait_send()
+        if 1 <= piece < npiece - 1:
+            next_pieces(piece + 1)
+        for index in range(len(offsets)):
+            vcopy(piece, index).wait_recv()
+        handle(piece + 1, arrived[piece].reshape(len(offsets) * prows, -1))
+        gather(piece)
+    gather(npiece)
+    out_ref[...] = total[...].T
+    for index in range(len(offsets)):
+        vcopy(npiece - 1, index).wait_send()
+    for group in range(npiece + 1):
+        for distance in distances:
+            partial_copy(group, distance).wait_send()
 
 
 def shards(nmode, nsite, w_modes, v_modes, momenta):
@@ -210,16 +224,18 @@
             pltpu.VMEM((PIECES, 2, nsc, prows, sites), jnp.bfloat16),
             pltpu.SMEM((nph, 3), jnp.int32),
             pltpu.VMEM((PIECES, prows, width), jnp.bfloat16),
-            pltpu.VMEM((nblocks, PIECES, prows, width), jnp.bfloat16),
+            pltpu.VMEM((PIECES, 2 * reach, prows, width), jnp.bfloat16),
             pltpu.VMEM((nsite, width, lanes), jnp.bfloat16),
-            pltpu.VMEM((nblocks, PIECES, nsite - 1, prows, lanes), jnp.bfloat16),
-            pltpu.VMEM((nblocks, PIECES, nsite - 1, prows, lanes), jnp.bfloat16),
-            pltpu.VMEM((nblocks, PIECES, prows, lanes), jnp.float32),
+            pltpu.VMEM((nblocks * vrows, lanes), jnp.float32),
+            pltpu.VMEM((nsite - 1, vrows, lanes), jnp.bfloat16),
+            pltpu.VMEM((PIECES, nsite - 1, 2 * reach * prows, lanes), jnp.bfloat16),
+            pltpu.VMEM((nsite - 1, vrows, lanes), jnp.bfloat16),
+            pltpu.VMEM((PIECES, nsite - 1, 2 * reach * prows, lanes), jnp.bfloat16),
             pltpu.SemaphoreType.DMA((2 + PIECES,)),
-            pltpu.SemaphoreType.DMA((nblocks, PIECES)),
-            pltpu.SemaphoreType.DMA((nblocks, PIECES)),
-            pltpu.SemaphoreType.DMA((nblocks, PIECES, nsite - 1)),
-            pltpu.SemaphoreType.DMA((nblocks, PIECES, nsite - 1)),
+            pltpu.SemaphoreType.DMA((PIECES, 2 * reach)),
+            pltpu.SemaphoreType.DMA((PIECES, 2 * reach)),
+            pltpu.SemaphoreType.DMA((PIECES + 1, nsite - 1)),
+            pltpu.SemaphoreType.DMA((PIECES + 1, nsite - 1)),
         ],
         compiler_params=pltpu.CompilerParams(
             collective_id=0, has_side_effects=True, vmem_limit_bytes=32 * 1024 * 1024

time: 21.3 us -> 18.9 us (0.89)
  Pallas kernels: 20.5 us -> 18.1 us
    pallas_call x1, Pallas kernels: 20.5 us -> 18.1 us  [shards(): pl.pallas_call(functools.partial(kernel, nmode, nsite, reach), out_shape=...]
where the time goes in v4:
time: 18.9 us; the launch traced here: 18.8 us
  Pallas kernels  18.1 us (96%)
  local copies, waits for them, and re-layouts  0.71 us (4%)
    pallas_call x1, Pallas kernels, shards(): pl.pallas_call(functools.partial(kernel, nmode, nsite, reach), out_shape=...  18.1 us
    unnamed x1, local copies, waits for them, and re-layouts  0.71 us

profile of v4, /device:TPU:0, one launch (start us, length us, event | category | flops | bytes accessed | tf_op | source)
XLA Modules:
  0.0 18.8 jit_solution(10359488841503069287)
XLA Ops:
  0.0 18.1 %shard_map.37 = f32[256,192]{1,0:T(8,128)S(1)} custom-call(bf16[2,12,64,128]{3,2,1,0:T(8,128)(2,1)} %bitcast.4, bf16[2,12,64,64]{3,2,1,0:T(8,128)(2,1)} %bitcast.5, s32[4,3]{1,0:T(4,128)} %mom_hbm.1), custom_call_target="tpu_custom_call" | custom-call | tf_op jit(solution)/shard_map/pallas_call | solution.py:213
  18.1 0.7 %copy.5 = f32[2,4,32,192]{3,2,1,0:T(8,128)} copy(f32[2,4,32,192]{3,2,1,0:T(8,128)S(1)} %bitcast.3) | data formatting | bytes 393216

commit v5 on v4

--- a/solution.py
+++ b/solution.py
@@ -81,15 +81,29 @@
             barrier, inc=1, device_id={"site": site_of(distance)}, device_id_type=MESH
         )
 
+    def offset_at(index):
+        return index - reach + jnp.where(index >= reach, 1, 0)
+
     def vcopy(piece, index):
         return pltpu.make_async_remote_copy(
             src_ref=packed.at[piece],
             dst_ref=arrived.at[piece, index],
             send_sem=vsend_sem.at[piece, index],
             recv_sem=vrecv_sem.at[piece, index],
-            device_id=mode_of(-offsets[index]),
+            device_id=mode_of(-offset_at(index)),
             device_id_type=MESH,
         )
+
+    if reach == 1 and npiece == 2:
+        last = mode == nmode - 1
+        end = (mode == 0) | last
+        around = jnp.where(last, 0, 1)
+        stages = [
+            [(0, jnp.where(end, around, 0)), (jnp.where(end, 1, 0), jnp.where(end, around, 1))],
+            [(jnp.where(end, 0, 1), jnp.where(end, 1 - around, 0)), (1, jnp.where(end, 1 - around, 1))],
+        ]
+    else:
+        stages = [[(piece, index) for index in range(len(offsets))] for piece in range(npiece)]
 
     for piece in range(npiece):
         load_v(piece).wait()
@@ -97,15 +111,12 @@
             packed[piece, :, sc * 2 * sites : (sc + 1) * 2 * sites] = jnp.concatenate(
                 [v_ref[piece, 0, sc], v_ref[piece, 1, sc]], axis=1
             )
-        if piece == 0:
-            pl.semaphore_wait(barrier, len(offsets) + nsite - 1)
-            for index in range(len(offsets)):
-                vcopy(piece, index).start()
+    pl.semaphore_wait(barrier, len(offsets) + nsite - 1)
+    for piece, index in stages[0]:
+        vcopy(piece, index).start()
 
     load_mom.wait()
     cosine, sine = phase_table(mom_ref, nph, rows, sites)
-    cosine = jnp.concatenate([cosine] * nsite, axis=1)
-    sine = jnp.concatenate([sine] * nsite, axis=1)
     shape = (wrows, nsite * half)
     mode_row = lax.broadcasted_iota(jnp.int32, shape, 0)
     lane = lax.broadcasted_iota(jnp.int32, shape, 1)
@@ -118,22 +129,26 @@
 
     load_w.wait()
     colours = nsc // SPINS
-    for sc in range(nsc):
-        spin, colour = sc // colours, sc % colours
-        sign = SIGNS[spin]
-        source = colours * (SPINS - 1 - spin) + colour
-        wreal = jnp.dot(w_ref[0, source], spread, preferred_element_type=jnp.float32)
-        wimag = jnp.dot(w_ref[1, source], spread, preferred_element_type=jnp.float32)
-        areal = (sign * (wreal * cosine + wimag * sine)).astype(jnp.bfloat16)
-        aimag = (sign * (wreal * sine - wimag * cosine)).astype(jnp.bfloat16)
-        top = pl.ds(sc * 2 * sites, sites)
-        low = pl.ds(sc * 2 * sites + sites, sites)
-        for s in range(nsite):
-            part = slice(s * half, (s + 1) * half)
-            lhs[s, top, 0:half] = areal[:, part]
-            lhs[s, top, half : 2 * half] = aimag[:, part]
-            lhs[s, low, 0:half] = -aimag[:, part]
-            lhs[s, low, half : 2 * half] = areal[:, part]
+    for spin in range(SPINS):
+        taken = slice(colours * (SPINS - 1 - spin), colours * (SPINS - spin))
+        both = jnp.concatenate(
+            [w_ref[part, taken].reshape(colours * sites, wrows) for part in range(2)], axis=0
+        )
+        wide = jnp.dot(both, spread, preferred_element_type=jnp.float32)
+        scos, ssin = SIGNS[spin] * cosine, SIGNS[spin] * sine
+        for colour in range(colours):
+            wreal = wide[colour * sites : (colour + 1) * sites]
+            wimag = wide[(colours + colour) * sites : (colours + colour + 1) * sites]
+            base = (colours * spin + colour) * 2 * sites
+            top, low = pl.ds(base, sites), pl.ds(base + sites, sites)
+            for s in range(nsite):
+                part = slice(s * half, (s + 1) * half)
+                areal = wreal[:, part] * scos + wimag[:, part] * ssin
+                aimag = wreal[:, part] * ssin - wimag[:, part] * scos
+                lhs[s, top, 0:half] = areal.astype(jnp.bfloat16)
+                lhs[s, top, half : 2 * half] = aimag.astype(jnp.bfloat16)
+                lhs[s, low, 0:half] = (-aimag).astype(jnp.bfloat16)
+                lhs[s, low, half : 2 * half] = areal.astype(jnp.bfloat16)
 
     distances = list(range(nsite - 1, 0, -1))
     if nsite > 2:
@@ -177,24 +192,25 @@
                 value = value + incoming[group][distance - 1, start:stop].astype(jnp.float32)
             total[column : column + stop - start, :] = value
 
-    def next_pieces(piece):
-        for index in range(len(offsets)):
-            vcopy(piece - 1, index).wait_send()
+    def next_stage(stage):
+        for piece, index in stages[stage - 1]:
+            vcopy(piece, index).wait_send()
+        for piece, index in stages[stage]:
             vcopy(piece, index).start()
 
-    next_pieces(1)
+    next_stage(1)
     handle(0, packed[...].reshape(vrows, -1))
     for piece in range(npiece):
         if 1 <= piece < npiece - 1:
-            next_pieces(piece + 1)
+            next_stage(piece + 1)
         for index in range(len(offsets)):
             vcopy(piece, index).wait_recv()
         handle(piece + 1, arrived[piece].reshape(len(offsets) * prows, -1))
         gather(piece)
     gather(npiece)
     out_ref[...] = total[...].T
-    for index in range(len(offsets)):
-        vcopy(npiece - 1, index).wait_send()
+    for piece, index in stages[-1]:
+        vcopy(piece, index).wait_send()
     for group in range(npiece + 1):
         for distance in distances:
             partial_copy(group, distance).wait_send()

time: 18.9 us -> 19 us (level)
  no operation moved by 1% of the time
where the time goes in v5:
time: 19 us; the launch traced here: 18.9 us
  Pallas kernels  18.2 us (96%)
  local copies, waits for them, and re-layouts  0.71 us (4%)
    pallas_call x1, Pallas kernels, shards(): pl.pallas_call(functools.partial(kernel, nmode, nsite, reach), out_shape=...  18.2 us
    unnamed x1, local copies, waits for them, and re-layouts  0.71 us

profile of v5, /device:TPU:0, one launch (start us, length us, event | category | flops | bytes accessed | tf_op | source)
XLA Modules:
  0.0 18.9 jit_solution(17209949829616643986)
XLA Ops:
  0.0 18.2 %shard_map.37 = f32[256,192]{1,0:T(8,128)S(1)} custom-call(bf16[2,12,64,128]{3,2,1,0:T(8,128)(2,1)} %bitcast.4, bf16[2,12,64,64]{3,2,1,0:T(8,128)(2,1)} %bitcast.5, s32[4,3]{1,0:T(4,128)} %mom_hbm.1), custom_call_target="tpu_custom_call" | custom-call | tf_op jit(solution)/shard_map/pallas_call | solution.py:229
  18.2 0.7 %copy.5 = f32[2,4,32,192]{3,2,1,0:T(8,128)} copy(f32[2,4,32,192]{3,2,1,0:T(8,128)S(1)} %bitcast.3) | data formatting | bytes 393216

commit v6 on v5

--- a/solution.py
+++ b/solution.py
@@ -105,15 +105,18 @@
     else:
         stages = [[(piece, index) for index in range(len(offsets))] for piece in range(npiece)]
 
+    sends = [send for stage in stages for send in stage]
     for piece in range(npiece):
         load_v(piece).wait()
         for sc in range(nsc):
             packed[piece, :, sc * 2 * sites : (sc + 1) * 2 * sites] = jnp.concatenate(
                 [v_ref[piece, 0, sc], v_ref[piece, 1, sc]], axis=1
             )
-    pl.semaphore_wait(barrier, len(offsets) + nsite - 1)
-    for piece, index in stages[0]:
-        vcopy(piece, index).start()
+        if piece == 0:
+            pl.semaphore_wait(barrier, len(offsets) + nsite - 1)
+            vcopy(*sends[0]).start()
+    for send in sends[1:]:
+        vcopy(*send).start()
 
     load_mom.wait()
     cosine, sine = phase_table(mom_ref, nph, rows, sites)
@@ -192,25 +195,16 @@
                 value = value + incoming[group][distance - 1, start:stop].astype(jnp.float32)
             total[column : column + stop - start, :] = value
 
-    def next_stage(stage):
-        for piece, index in stages[stage - 1]:
-            vcopy(piece, index).wait_send()
-        for piece, index in stages[stage]:
-            vcopy(piece, index).start()
-
-    next_stage(1)
     handle(0, packed[...].reshape(vrows, -1))
     for piece in range(npiece):
-        if 1 <= piece < npiece - 1:
-            next_stage(piece + 1)
         for index in range(len(offsets)):
             vcopy(piece, index).wait_recv()
         handle(piece + 1, arrived[piece].reshape(len(offsets) * prows, -1))
         gather(piece)
     gather(npiece)
     out_ref[...] = total[...].T
-    for piece, index in stages[-1]:
-        vcopy(piece, index).wait_send()
+    for send in sends:
+        vcopy(*send).wait_send()
     for group in range(npiece + 1):
         for distance in distances:
             partial_copy(group, distance).wait_send()

time: 19 us -> 18.9 us (level)
  Pallas kernels: 18.2 us -> 18 us
where the time goes in v6:
time: 18.9 us; the launch traced here: 18.8 us
  Pallas kernels  18 us (95%)
  local copies, waits for them, and re-layouts  0.71 us (4%)
    pallas_call x1, Pallas kernels, shards(): pl.pallas_call(functools.partial(kernel, nmode, nsite, reach), out_shape=...  18 us
    unnamed x1, local copies, waits for them, and re-layouts  0.71 us

profile of v6, /device:TPU:0, one launch (start us, length us, event | category | flops | bytes accessed | tf_op | source)
XLA Modules:
  0.0 18.8 jit_solution(17712102409983997282)
XLA Ops:
  0.0 18.0 %shard_map.37 = f32[256,192]{1,0:T(8,128)S(1)} custom-call(bf16[2,12,64,128]{3,2,1,0:T(8,128)(2,1)} %bitcast.4, bf16[2,12,64,64]{3,2,1,0:T(8,128)(2,1)} %bitcast.5, s32[4,3]{1,0:T(4,128)} %mom_hbm.1), custom_call_target="tpu_custom_call" | custom-call | tf_op jit(solution)/shard_map/pallas_call | solution.py:223
  18.0 0.7 %copy.5 = f32[2,4,32,192]{3,2,1,0:T(8,128)} copy(f32[2,4,32,192]{3,2,1,0:T(8,128)S(1)} %bitcast.3) | data formatting | bytes 393216

commit v7 on v6

--- a/solution.py
+++ b/solution.py
@@ -11,7 +11,7 @@
 LAT = 96
 REACH = 4
 SPINS = 4
-PIECES = 2
+PIECES = 1
 SIGNS = (-1.0, 1.0, 1.0, -1.0)
 MESH = pl.DeviceIdType.MESH
 

time: 18.9 us -> 18.8 us (level)
  Pallas kernels: 18 us -> 17.8 us
    pallas_call x1, Pallas kernels: 18 us -> 17.8 us  [shards(): pl.pallas_call(functools.partial(kernel, nmode, nsite, reach), out_shape=...]
where the time goes in v7:
time: 18.8 us; the launch traced here: 18.5 us
  Pallas kernels  17.8 us (95%)
  local copies, waits for them, and re-layouts  0.71 us (4%)
    pallas_call x1, Pallas kernels, shards(): pl.pallas_call(functools.partial(kernel, nmode, nsite, reach), out_shape=...  17.8 us
    unnamed x1, local copies, waits for them, and re-layouts  0.71 us

profile of v7, /device:TPU:0, one launch (start us, length us, event | category | flops | bytes accessed | tf_op | source)
XLA Modules:
  0.0 18.5 jit_solution(16604984869396534919)
XLA Ops:
  0.0 17.8 %shard_map.37 = f32[256,192]{1,0:T(8,128)S(1)} custom-call(bf16[2,12,64,128]{3,2,1,0:T(8,128)(2,1)} %bitcast.4, bf16[2,12,64,64]{3,2,1,0:T(8,128)(2,1)} %bitcast.5, s32[4,3]{1,0:T(4,128)} %mom_hbm.1), custom_call_target="tpu_custom_call" | custom-call | tf_op jit(solution)/shard_map/pallas_call | solution.py:223
  17.8 0.7 %copy.5 = f32[2,4,32,192]{3,2,1,0:T(8,128)} copy(f32[2,4,32,192]{3,2,1,0:T(8,128)S(1)} %bitcast.3) | data formatting | bytes 393216

commit v8 on v7

--- a/solution.py
+++ b/solution.py
@@ -102,6 +102,9 @@
             [(0, jnp.where(end, around, 0)), (jnp.where(end, 1, 0), jnp.where(end, around, 1))],
             [(jnp.where(end, 0, 1), jnp.where(end, 1 - around, 0)), (1, jnp.where(end, 1 - around, 1))],
         ]
+    elif reach == 1 and npiece == 1:
+        around = jnp.where(mode == nmode - 1, 0, 1)
+        stages = [[(0, around), (0, 1 - around)]]
     else:
         stages = [[(piece, index) for index in range(len(offsets))] for piece in range(npiece)]
 

time: 18.8 us -> 18.9 us (level)
  no operation moved by 1% of the time
where the time goes in v8:
time: 18.9 us; the launch traced here: 18.5 us
  Pallas kernels  17.8 us (94%)
  local copies, waits for them, and re-layouts  0.71 us (4%)
    pallas_call x1, Pallas kernels, shards(): pl.pallas_call(functools.partial(kernel, nmode, nsite, reach), out_shape=...  17.8 us
    unnamed x1, local copies, waits for them, and re-layouts  0.71 us

profile of v8, /device:TPU:0, one launch (start us, length us, event | category | flops | bytes accessed | tf_op | source)
XLA Modules:
  0.0 18.5 jit_solution(14849349324130569573)
XLA Ops:
  0.0 17.8 %shard_map.37 = f32[256,192]{1,0:T(8,128)S(1)} custom-call(bf16[2,12,64,128]{3,2,1,0:T(8,128)(2,1)} %bitcast.4, bf16[2,12,64,64]{3,2,1,0:T(8,128)(2,1)} %bitcast.5, s32[4,3]{1,0:T(4,128)} %mom_hbm.1), custom_call_target="tpu_custom_call" | custom-call | tf_op jit(solution)/shard_map/pallas_call | solution.py:226
  17.8 0.7 %copy.5 = f32[2,4,32,192]{3,2,1,0:T(8,128)} copy(f32[2,4,32,192]{3,2,1,0:T(8,128)S(1)} %bitcast.3) | data formatting | bytes 393216
